TPU v7x, 32 devices: a whole 2x2x4 slice. The times are simulated.
32 devices in a mesh: lat: 8 (over z, x), deg: 4 (over y, core).
Axes of the slice: x: 2, y: 2, z: 4, core: 2. Of those that a mesh axis runs over, the one named last changes fastest.
Arguments:
- eta_tl: float32 [64, 10752], P('lat'), may hold values from -6 to 6
- vel_tl: float32 [2, 64, 10752], P(None, 'lat'), may hold values from -6 to 6
- eta_adj: float32 [64, 10752], P('lat'), may hold values from -6 to 6
- vel_adj: float32 [2, 64, 10752], P(None, 'lat'), may hold values from -6 to 6
- depth: float32 [64, 10752], P('lat'), may hold values from 0.2 to 1
- drag: float32 [64, 10752], P('lat'), may hold values from 0.01 to 0.3
- ocean: int32 [64, 10752], P('lat'), may hold values 0 or 1
- basis: bfloat16 [1024, 64, 1024], P('lat', None, 'deg'), may hold values from -5 to 5
- love: float32 [1024], P('deg'), may hold values from 0.05 to 0.5
Outputs:
- eta_tl_out: float32 [64, 10752], P('lat')
- vel_tl_out: float32 [2, 64, 10752], P(None, 'lat')
- eta_adj_out: float32 [64, 10752], P('lat')
- vel_adj_out: float32 [2, 64, 10752], P(None, 'lat')
All inputs are finite; a program needn't handle non-finite values. No bound on the sum of `ocean` on one device may be relied on, other than what follows from the above.
Results may differ from a plain program's by a relative error of at most 0.02.
Values may be sent and summed in bfloat16 or wider, within the bound.
A program may use at most 320 MiB of HBM per device.

v0:
```python
import jax
import jax.numpy as jnp
import numpy as np
from jax import lax
from jax.sharding import PartitionSpec as P

STEPS = 2
LANES = 128
kappa_x = 0.3
kappa_y = 0.4


def passed_along(value, axis, by):
    length = lax.axis_size(axis)
    pairs = [(i, i + by) for i in range(length) if 0 <= i + by < length]
    return lax.ppermute(value, axis, pairs)


def circle(numerator, period):
    angles = 2.0 * np.pi * (numerator % period) / period
    return (np.cos(angles), np.sin(angles))


def fourier_tables(lon_count, order_total):
    major = lon_count // LANES
    blocks = -(-order_total // major)
    residues, lanes = (np.arange(major), np.arange(LANES))
    outer = np.stack(circle(residues[:, None] * residues[None, :], major))
    turn = np.stack(circle(residues[:, None] * lanes[None, :], lon_count))
    inner = np.stack(circle(np.arange(blocks)[:, None] * lanes[None, :], LANES))
    return (
        jnp.asarray(outer, jnp.bfloat16),
        jnp.asarray(turn, jnp.float32),
        jnp.asarray(inner, jnp.bfloat16),
    )


def order_factor(orders):
    return jnp.where(orders == 0, 1.0, 2.0).astype(jnp.bfloat16)


def analyse(stacked, analysis_weight, tables, order_count):
    outer, turn, inner = tables
    row_count = stacked.shape[1]
    lon_count = stacked.shape[2]
    split_rows = stacked.astype(jnp.bfloat16).reshape(2 * row_count, lon_count // LANES, LANES)
    first = jnp.einsum("cka,rab->crkb", outer, split_rows, preferred_element_type=jnp.float32)
    turned = jnp.stack(
        [first[0] * turn[0] - first[1] * turn[1], first[1] * turn[0] + first[0] * turn[1]]
    ).astype(jnp.bfloat16)
    second = jnp.stack([jnp.stack([inner[0], -inner[1]]), jnp.stack([inner[1], inner[0]])])
    spectra = jnp.einsum("crkb,dcnb->dnkr", turned, second, preferred_element_type=jnp.float32)
    spectra = spectra.reshape(2, -1, 2, row_count)[:, :order_count] * (1.0 / lon_count)
    return (spectra * analysis_weight[None, None, :, :]).astype(jnp.bfloat16)


def legendre(spectra, basis, love):
    coeffs = jnp.einsum("cmfi,mil->cmfl", spectra, basis, preferred_element_type=jnp.float32)
    scaled = (coeffs * love[None, None, None, :]).astype(jnp.bfloat16)
    return jnp.einsum("cmfl,mil->cmfi", scaled, basis, preferred_element_type=jnp.float32)


def synthesise(coeffs, factors, tables, output_weight):
    outer, turn, inner = tables
    major, blocks = (turn.shape[1], inner.shape[1])
    order_count = coeffs.shape[1]
    row_count = coeffs.shape[3]
    scaled = coeffs * factors[None, :, None, None]
    padded = jnp.pad(scaled, ((0, 0), (0, major * blocks - order_count), (0, 0), (0, 0)))
    padded = padded.reshape(2, blocks, major, 2 * row_count)
    second = jnp.stack([jnp.stack([inner[0], inner[1]]), jnp.stack([-inner[1], inner[0]])])
    first = jnp.einsum("cnkr,dcnb->drkb", padded, second, preferred_element_type=jnp.float32)
    turned = jnp.stack(
        [first[0] * turn[0] + first[1] * turn[1], first[1] * turn[0] - first[0] * turn[1]]
    ).astype(jnp.bfloat16)
    grid_out = jnp.einsum("cka,crkb->rab", outer, turned, preferred_element_type=jnp.float32)
    return grid_out.reshape(2, row_count, -1) * output_weight[:, :, None]


def edges_from(rows, by):
    sent = jnp.concatenate(rows, 0).astype(jnp.bfloat16)
    got = passed_along(sent, "lat", by).astype(jnp.float32)
    return [got[i : i + 1] for i in range(len(rows))]


def northward(values, edge):
    return jnp.concatenate([values[1:], edge], 0)


def southward(values, edge):
    return jnp.concatenate([edge, values[:-1]], 0)


def on_device(eta_tl, vel_tl, eta_adj, vel_adj, depth, drag, ocean, basis, love):
    row_count = eta_tl.shape[0]
    lon_count = eta_tl.shape[1]
    lat_count = lax.axis_size("lat")
    total_rows = row_count * lat_count
    first_row = lax.axis_index("lat") * row_count
    indices = first_row + jnp.arange(row_count, dtype=jnp.int32)
    latitude = (indices.astype(jnp.float32) + 0.5) * (jnp.pi / total_rows) - 0.5 * jnp.pi
    cosine = jnp.cos(latitude)
    quad_weight = jnp.pi / total_rows * cosine
    east_factor = (kappa_x / (0.5 + 0.5 * cosine))[:, None]
    wet_mask = ocean.astype(jnp.float32)
    flux_north = kappa_y * wet_mask * eta_adj
    north_depth, north_wet, north_flux = edges_from([depth[:1], wet_mask[:1], flux_north[:1]], -1)
    depth_up = northward(depth, north_depth)
    wet_up = northward(wet_mask, north_wet)
    mask_u = wet_mask * jnp.roll(wet_mask, -1, 1)
    mask_v = wet_mask * wet_up
    depth_u = 0.5 * (depth + jnp.roll(depth, -1, 1))
    depth_v = 0.5 * (depth + depth_up)
    retain = 1.0 - drag
    ones_weight = jnp.ones_like(quad_weight)
    analysis_weight = jnp.stack([quad_weight, ones_weight])
    output_weight = jnp.stack([ones_weight, quad_weight])
    owned_count = basis.shape[0]
    order_total = owned_count * lat_count
    full_orders = jnp.arange(order_total, dtype=jnp.int32)
    tables = fourier_tables(lon_count, order_total)
    full_factor = order_factor(full_orders)
    state_eta, state_vel = (eta_tl, vel_tl)
    back_eta, back_vel = (eta_adj, vel_adj)

    def adjoint_terms(eta, vel, flux_edge):
        flux_east = east_factor * wet_mask * eta
        flux_up = kappa_y * wet_mask * eta
        north_up = northward(flux_up, flux_edge)
        p_term = mask_u * (vel[0] + depth_u * (jnp.roll(flux_east, -1, 1) - flux_east))
        q_term = mask_v * (vel[1] + depth_v * (north_up - flux_up))
        return (p_term, q_term)

    p_term, q_term = adjoint_terms(back_eta, back_vel, north_flux)
    (q_edge,) = edges_from([q_term[-1:]], 1)
    for step_index in range(STEPS):
        flux_p = east_factor * p_term
        q_down = southward(q_term, q_edge)
        psi_bar = flux_p - jnp.roll(flux_p, 1, 1) + kappa_y * (q_term - q_down)
        spectra = analyse(jnp.stack([state_eta, psi_bar]), analysis_weight, tables, order_total)
        owned_rows = lax.all_to_all(spectra, "lat", split_axis=1, concat_axis=3, tiled=True)
        partial_value = legendre(owned_rows, basis, love)
        total_sum = lax.psum(partial_value.astype(jnp.bfloat16), "deg")
        banded = lax.all_to_all(total_sum, "lat", split_axis=3, concat_axis=1, tiled=True)
        loads = synthesise(banded, full_factor, tables, output_weight)
        last = step_index == STEPS - 1
        psi_now = state_eta - loads[0]
        back_eta = back_eta + psi_bar - loads[1]
        back_vel = (retain * p_term, retain * q_term)
        north_rows = [psi_now[:1]]
        if not last:
            north_rows.append(kappa_y * wet_mask[:1] * back_eta[:1])
        north_edges = edges_from(north_rows, -1)
        psi_up = northward(psi_now, north_edges[0])
        new_u = mask_u * (
            retain * state_vel[0] - east_factor * (jnp.roll(psi_now, -1, 1) - psi_now)
        )
        new_v = mask_v * (retain * state_vel[1] - kappa_y * (psi_up - psi_now))
        flux_x = depth_u * new_u
        flux_y = depth_v * new_v
        south_rows = [flux_y[-1:]]
        if not last:
            p_term, q_term = adjoint_terms(back_eta, back_vel, north_edges[1])
            south_rows.append(q_term[-1:])
        south_edges = edges_from(south_rows, 1)
        flux_down = southward(flux_y, south_edges[0])
        if not last:
            q_edge = south_edges[1]
        state_eta = state_eta - wet_mask * (
            east_factor * (flux_x - jnp.roll(flux_x, 1, 1)) + kappa_y * (flux_y - flux_down)
        )
        state_vel = (new_u, new_v)
    state_vel, back_vel = (jnp.stack(state_vel), jnp.stack(back_vel))
    return (state_eta, state_vel, back_eta, back_vel)


def solution(mesh):
    in_specs = (
        P("lat", None),
        P(None, "lat", None),
        P("lat", None),
        P(None, "lat", None),
        P("lat", None),
        P("lat", None),
        P("lat", None),
        P("lat", None, "deg"),
        P("deg"),
    )
    out_specs = (P("lat", None), P(None, "lat", None), P("lat", None), P(None, "lat", None))
    return jax.shard_map(
        on_device, mesh=mesh, in_specs=in_specs, out_specs=out_specs, check_vma=False
    )
```

profile of v0, /device:TPU:0, one launch (start us, length us, event | category | flops | bytes accessed | tf_op | source)
XLA Modules:
  0.0 200.0 jit_solution(16623130963314955521)
XLA Ops:
  7.3 1.0 slice.442
  8.3 1.0 convert_element_type.99
  9.3 1.3 multiply_multiply_fusion.3
  10.8 1.3 collective-permute-start
  12.8 0.5 copy-done.4
  13.4 4.8 %collective-permute-done = bf16[3,10752]{1,0:T(4,128)(2,1)S(1)} collective-permute-done((bf16[3,10752]{1,0:T(4,128)(2,1)S(1)}, bf16[3,10752]{1,0:T(4,128)(2,1)S(1)}, u32[]{:S(2)}, u32[]{:S(2)}) %collective-permute-start) | collective-permute-done | bytes 64544 | tf_op jit(solution)/shard_map/ppermute | solution.py:16
  18.3 1.3 broadcast_multiply_fusion.3
  19.7 4.8 %collective-permute-start.1 = (bf16[1,10752]{1,0:T(2,128)(2,1)S(1)}, bf16[1,10752]{1,0:T(2,128)(2,1)S(1)}, u32[]{:S(2)}, u32[]{:S(2)}) collective-permute-start(bf16[1,10752]{1,0:T(2,128)(2,1)S(1)} %slice.440), channel_id=1, source_target_pairs={{0,4},{4,8},{8,12},{12,16},{16,20},{20,24},{24,28},{1,5},{5,9},{9,... | collective-permute-start | bytes 64520 | tf_op jit(solution)/shard_map/ppermute | solution.py:16
  24.6 1.6 collective-permute-done.1
  26.2 0.9 convert_bitcast_fusion.2
  27.4 0.3 convolution_bitcast_fusion.3
  27.7 0.2 copy-done.19
  28.1 0.5 copy-done.33
  28.7 0.4 convolution_bitcast_fusion.7
  29.3 0.7 copy.57
  30.0 1.1 reshape.104
  31.1 12.4 %all_to_all.72 = bf16[8,2,2048]{2,1,0:T(2,128)(2,1)S(1)} all-to-all(bf16[8,2,2048]{2,1,0:T(2,128)(2,1)S(1)} %reshape.104), channel_id=1, replica_groups=mesh['lat'=8,'deg'=4] {'lat'}, dimensions={0} | all-to-all | bytes 131072 | tf_op jit(solution)/shard_map/all_to_all | solution.py:141
  43.5 1.2 reshape.105
  44.7 1.3 copy.90
  46.2 6.0 %fusion.45 = bf16[2,128,2,64]{3,2,0,1:T(2,128)(2,1)} fusion(bf16[128,64,256]{2,1,0:T(8,128)(2,1)} %param.19, bf16[2,128,2,64]{3,2,0,1:T(2,128)(2,1)S(1)} %copy.60, f32[256]{0:T(256)S(1)} %copy-done.31), kind=kOutput, calls=%fused_computation.25 | convolution fusion | flops 33849344 | bytes 4326400 | tf_op jit(solution)/shard_map/cmfl,mil->cmfi/dot_general | solution.py:60
  52.2 29.1 %all-reduce.7.cloned.1.call-done = bf16[2,128,2,64]{3,2,0,1:T(2,128)(2,1)} async-done(((bf16[2,128,2,64]{3,2,0,1:T(2,128)(2,1)}), bf16[2,128,2,64]{3,2,0,1:T(2,128)(2,1)}) %all-reduce.7.cloned.1.call-update) | async-done | bytes 65552 | tf_op jit(solution)/shard_map/psum | solution.py:143
  81.3 1.7 copy.61
  83.0 5.5 %all-to-all-start.1 = ((bf16[2,128,2,64]{1,2,0,3:T(2,128)(2,1)}), bf16[2,128,2,64]{1,2,0,3:T(2,128)(2,1)S(1)}, u32[]{:S(2)}, u32[]{:S(2)}) async-start(bf16[2,128,2,64]{1,2,0,3:T(2,128)(2,1)} %copy.61), calls=%async_computation.1 | async-start | bytes 131072 | tf_op jit(solution)/shard_map/all_to_all | solution.py:144
  88.5 6.8 %all-to-all-done.1 = bf16[2,128,2,64]{1,2,0,3:T(2,128)(2,1)S(1)} async-done(((bf16[2,128,2,64]{1,2,0,3:T(2,128)(2,1)}), bf16[2,128,2,64]{1,2,0,3:T(2,128)(2,1)S(1)}, u32[]{:S(2)}, u32[]{:S(2)}) %all-to-all-start.1) | async-done | bytes 65568 | tf_op jit(solution)/shard_map/all_to_all | solution.py:144
  95.4 0.2 reshape.79
  95.6 0.4 convolution_bitcast_fusion.2
  96.2 0.3 convolution_bitcast_fusion.5
  96.8 0.8 copy-done.12
  98.0 0.7 copy-done.2
  98.9 1.3 collective-permute-start.2
  100.2 0.9 multiply_bitcast_fusion.1
  101.4 3.5 %collective-permute-done.2 = bf16[2,10752]{1,0:T(2,128)(2,1)S(1)} collective-permute-done((bf16[2,10752]{1,0:T(2,128)(2,1)S(1)}, bf16[2,10752]{1,0:T(2,128)(2,1)S(1)}, u32[]{:S(2)}, u32[]{:S(2)}) %collective-permute-start.2) | collective-permute-done | bytes 43040 | tf_op jit(solution)/shard_map/ppermute | solution.py:16
  104.9 1.3 fusion.128
  106.5 3.4 %collective-permute-start.3 = (bf16[2,10752]{1,0:T(2,128)(2,1)S(1)}, bf16[2,10752]{1,0:T(2,128)(2,1)S(1)}, u32[]{:S(2)}, u32[]{:S(2)}) collective-permute-start(bf16[2,10752]{1,0:T(2,128)(2,1)S(1)} %pad_maximum_fusion.6), channel_id=1, source_target_pairs={{0,4},{4,8},{8,12},{12,16},{16,20},{20,24},{24,28},{1,5},{5,9},{9,... | collective-permute-start | bytes 129032 | tf_op jit(solution)/shard_map/ppermute | solution.py:16
  110.0 1.3 collective-permute-done.3
  111.4 0.2 convert_bitcast_fusion.1
  112.1 0.3 convolution_bitcast_fusion.1
  112.4 0.3 copy-done.21
  112.9 0.5 copy-done.34
  113.4 0.4 convolution_bitcast_fusion.6
  114.0 0.7 copy.66
  114.7 1.1 reshape.106
  115.8 10.6 %all_to_all.73 = bf16[8,2,2048]{2,1,0:T(2,128)(2,1)S(1)} all-to-all(bf16[8,2,2048]{2,1,0:T(2,128)(2,1)S(1)} %reshape.106), channel_id=1, replica_groups=mesh['lat'=8,'deg'=4] {'lat'}, dimensions={0} | all-to-all | bytes 131072 | tf_op jit(solution)/shard_map/all_to_all | solution.py:141
  126.4 1.2 reshape.107
  127.6 1.3 copy.96
  129.1 6.0 %fusion.40 = bf16[2,128,2,64]{3,2,0,1:T(2,128)(2,1)} fusion(bf16[128,64,256]{2,1,0:T(8,128)(2,1)} %param.19, bf16[2,128,2,64]{3,2,0,1:T(2,128)(2,1)S(1)} %copy.69, f32[256]{0:T(256)S(1)} %copy-done.32), kind=kOutput, calls=%fused_computation.24 | convolution fusion | flops 33849344 | bytes 4326400 | tf_op jit(solution)/shard_map/cmfl,mil->cmfi/dot_general | solution.py:60
  135.1 28.1 %all-reduce.9.cloned.1.call-done = bf16[2,128,2,64]{3,2,0,1:T(2,128)(2,1)} async-done(((bf16[2,128,2,64]{3,2,0,1:T(2,128)(2,1)}), bf16[2,128,2,64]{3,2,0,1:T(2,128)(2,1)}) %all-reduce.9.cloned.1.call-update) | async-done | bytes 65552 | tf_op jit(solution)/shard_map/psum | solution.py:143
  163.2 1.0 copy.70
  164.3 12.2 %all_to_all.74 = bf16[2,128,2,64]{1,2,0,3:T(2,128)(2,1)S(1)} all-to-all(bf16[2,128,2,64]{1,2,0,3:T(2,128)(2,1)S(1)} %copy.70), channel_id=1, replica_groups=mesh['lat'=8,'deg'=4] {'lat'}, dimensions={3} | all-to-all | bytes 131072 | tf_op jit(solution)/shard_map/all_to_all | solution.py:144
  176.5 0.2 reshape.82
  176.7 0.4 convolution_bitcast_fusion
  177.2 0.2 add_convert_fusion
  177.4 0.3 convolution_bitcast_fusion.4
  177.7 1.0 reshape.83
  178.6 1.2 broadcast_multiply_fusion
  179.9 0.8 fusion.62
  180.8 1.4 collective-permute-start.4
  182.2 0.9 pad_maximum_fusion.1
  183.3 3.5 %collective-permute-done.4 = bf16[1,10752]{1,0:T(2,128)(2,1)S(1)} collective-permute-done((bf16[1,10752]{1,0:T(2,128)(2,1)S(1)}, bf16[1,10752]{1,0:T(2,128)(2,1)S(1)}, u32[]{:S(2)}, u32[]{:S(2)}) %collective-permute-start.4) | collective-permute-done | bytes 21536 | tf_op jit(solution)/shard_map/ppermute | solution.py:16
  186.9 0.3 fusion.119
  187.3 3.2 %collective-permute-start.5 = (bf16[1,10752]{1,0:T(2,128)(2,1)S(1)}, bf16[1,10752]{1,0:T(2,128)(2,1)S(1)}, u32[]{:S(2)}, u32[]{:S(2)}) collective-permute-start(bf16[1,10752]{1,0:T(2,128)(2,1)S(1)} %slice.435), channel_id=1, source_target_pairs={{0,4},{4,8},{8,12},{12,16},{16,20},{20,24},{24,28},{1,5},{5,9},{9,... | collective-permute-start | bytes 64520 | tf_op jit(solution)/shard_map/ppermute | solution.py:16
  190.5 0.9 pad_maximum_fusion
  191.4 0.7 collective-permute-done.5
  192.2 0.9 fusion.101
  (135 shorter events, 5.2 us)
Async XLA Ops:
  7.2 74.1 %all-reduce.7.cloned.1.call-start = ((), (), s32[]{:S(2)}) async-start(), calls=%async_computation.4 | async-start | bytes 262144 | tf_op jit(solution)/shard_map/psum | solution.py:143
  9.3 3.1 %copy-start.1 = (f32[8,10752]{1,0:T(8,128)}, f32[8,10752]{1,0:T(8,128)S(1)}, u32[]{:S(2)}) copy-start(f32[8,10752]{1,0:T(8,128)S(1)} %convert_element_type.99) | copy-start | bytes 1032196
  9.3 3.0 %copy-start.3 = (f32[8,10752]{1,0:T(8,128)S(1)}, f32[8,10752]{1,0:T(8,128)}, u32[]{:S(2)}) copy-start(f32[8,10752]{1,0:T(8,128)} %param.16) | copy-start | bytes 1032196
  10.8 7.4 %collective-permute-start = (bf16[3,10752]{1,0:T(4,128)(2,1)S(1)}, bf16[3,10752]{1,0:T(4,128)(2,1)S(1)}, u32[]{:S(2)}, u32[]{:S(2)}) collective-permute-start(bf16[3,10752]{1,0:T(4,128)(2,1)S(1)} %pad_maximum_fusion.4), channel_id=1, source_target_pairs={{4,0},{8,4},{12,8},{16,12},{20,16},{24,20},{28,24},{5,1},{9,5},{13... | collective-permute-start | bytes 193544 | tf_op jit(solution)/shard_map/ppermute | solution.py:16
  12.4 1.0 copy-start.4
  12.5 5.8 %copy-start = (s32[8,10752]{1,0:T(8,128)S(1)}, s32[8,10752]{1,0:T(8,128)}, u32[]{:S(2)}) copy-start(s32[8,10752]{1,0:T(8,128)} %param.18) | copy-start | bytes 1032196
  12.5 5.8 %slice-start = ((f32[8,10752]{1,0:T(8,128)}), f32[8,1]{1,0:T(8,128)S(1)}, s32[]{:S(2)}) async-start(f32[8,10752]{1,0:T(8,128)} %copy-done.1), calls=%async_computation.6 | async-start | bytes 8192 | tf_op jit(solution)/shard_map/jit(_roll_static)/slice | solution.py:110
  12.5 5.8 %slice-start.1 = ((f32[8,10752]{1,0:T(8,128)}), f32[8,1]{1,0:T(8,128)S(1)}, s32[]{:S(2)}) async-start(f32[8,10752]{1,0:T(8,128)} %param.16), calls=%async_computation.7 | async-start | bytes 8192 | tf_op jit(solution)/shard_map/jit(_roll_static)/slice | solution.py:112
  12.6 5.8 %copy-start.23 = (f32[2,8,10752]{2,1,0:T(8,128)S(1)}, f32[2,8,10752]{2,1,0:T(8,128)}, u32[]{:S(2)}) copy-start(f32[2,8,10752]{2,1,0:T(8,128)} %param.15) | copy-start | bytes 2064388
  19.7 6.4 %collective-permute-start.1 = (bf16[1,10752]{1,0:T(2,128)(2,1)S(1)}, bf16[1,10752]{1,0:T(2,128)(2,1)S(1)}, u32[]{:S(2)}, u32[]{:S(2)}) collective-permute-start(bf16[1,10752]{1,0:T(2,128)(2,1)S(1)} %slice.440), channel_id=1, source_target_pairs={{0,4},{4,8},{8,12},{12,16},{16,20},{20,24},{24,28},{1,5},{5,9},{9,... | collective-permute-start | bytes 64520 | tf_op jit(solution)/shard_map/ppermute | solution.py:16
  24.5 4.7 %copy-start.29 = (f32[2,8]{1,0:T(2,128)}, f32[2,8]{1,0:T(2,128)S(1)}, u32[]{:S(2)}) copy-start(f32[2,8]{1,0:T(2,128)S(1)} %get-tuple-element.62) | copy-start | bytes 196
  24.5 72.2 %copy-start.27 = (f32[2,8]{1,0:T(2,128)}, f32[2,8]{1,0:T(2,128)S(1)}, u32[]{:S(2)}) copy-start(f32[2,8]{1,0:T(2,128)S(1)} %get-tuple-element.61) | copy-start | bytes 196
  26.2 1.2 copy-start.18
  27.1 0.8 copy-start.19
  27.1 0.8 copy-start.20
  27.9 0.7 copy-start.33
  31.1 15.1 %copy-start.31 = (f32[256]{0:T(256)S(1)}, f32[256]{0:T(256)}, u32[]{:S(2)}) copy-start(f32[256]{0:T(256)} %param.20) | copy-start | bytes 3076
  46.1 49.5 %copy-start.25 = (bf16[2,2,13,128,1]{3,2,1,0,4:T(8,128)(2,1)S(1)}, bf16[2,2,13,128,1]{3,2,1,0,4:T(8,128)(2,1)}, u32[]{:S(2)}) copy-start(bf16[2,2,13,128,1]{3,2,1,0,4:T(8,128)(2,1)} %constant.67) | copy-start | bytes 39940
  83.0 12.4 %all-to-all-start.1 = ((bf16[2,128,2,64]{1,2,0,3:T(2,128)(2,1)}), bf16[2,128,2,64]{1,2,0,3:T(2,128)(2,1)S(1)}, u32[]{:S(2)}, u32[]{:S(2)}) async-start(bf16[2,128,2,64]{1,2,0,3:T(2,128)(2,1)} %copy.61), calls=%async_computation.1 | async-start | bytes 131072 | tf_op jit(solution)/shard_map/all_to_all | solution.py:144
  88.5 74.7 %all-reduce.9.cloned.1.call-start = ((), (), s32[]{:S(2)}) async-start(), calls=%async_computation.5 | async-start | bytes 262144 | tf_op jit(solution)/shard_map/psum | solution.py:143
  96.7 1.0 copy-start.12
  96.7 1.1 copy-start.13
  97.8 1.0 copy-start.2
  97.8 2.5 %copy-start.5 = (f32[8,10752]{1,0:T(8,128)S(1)}, f32[8,10752]{1,0:T(8,128)}, u32[]{:S(2)}) copy-start(f32[8,10752]{1,0:T(8,128)} %param.17) | copy-start | bytes 1032196
  97.8 2.5 %copy-start.17 = (f32[8,10752]{1,0:T(8,128)S(1)}, f32[8,10752]{1,0:T(8,128)}, u32[]{:S(2)}) copy-start(f32[8,10752]{1,0:T(8,128)} %get-tuple-element.28) | copy-start | bytes 1032196
  98.9 5.9 %collective-permute-start.2 = (bf16[2,10752]{1,0:T(2,128)(2,1)S(1)}, bf16[2,10752]{1,0:T(2,128)(2,1)S(1)}, u32[]{:S(2)}, u32[]{:S(2)}) collective-permute-start(bf16[2,10752]{1,0:T(2,128)(2,1)S(1)} %pad_maximum_fusion.5), channel_id=1, source_target_pairs={{4,0},{8,4},{12,8},{16,12},{20,16},{24,20},{28,24},{5,1},{9,5},{13... | collective-permute-start | bytes 129032 | tf_op jit(solution)/shard_map/ppermute | solution.py:16
  101.1 3.8 %copy-start.7 = (f32[8,10752]{1,0:T(8,128)S(1)}, f32[8,10752]{1,0:T(8,128)}, u32[]{:S(2)}) copy-start(f32[8,10752]{1,0:T(8,128)} %get-tuple-element.42) | copy-start | bytes 1032196
  101.1 3.8 %copy-start.9 = (f32[8,10752]{1,0:T(8,128)S(1)}, f32[8,10752]{1,0:T(8,128)}, u32[]{:S(2)}) copy-start(f32[8,10752]{1,0:T(8,128)} %get-tuple-element.43) | copy-start | bytes 1032196
  101.1 3.8 %copy-start.24 = (f32[2,8,10752]{2,1,0:T(8,128)S(1)}, f32[2,8,10752]{2,1,0:T(8,128)}, u32[]{:S(2)}) copy-start(f32[2,8,10752]{2,1,0:T(8,128)} %param.13) | copy-start | bytes 2064388
  106.5 4.9 %collective-permute-start.3 = (bf16[2,10752]{1,0:T(2,128)(2,1)S(1)}, bf16[2,10752]{1,0:T(2,128)(2,1)S(1)}, u32[]{:S(2)}, u32[]{:S(2)}) collective-permute-start(bf16[2,10752]{1,0:T(2,128)(2,1)S(1)} %pad_maximum_fusion.6), channel_id=1, source_target_pairs={{0,4},{4,8},{8,12},{12,16},{16,20},{20,24},{24,28},{1,5},{5,9},{9,... | collective-permute-start | bytes 129032 | tf_op jit(solution)/shard_map/ppermute | solution.py:16
  111.9 0.8 copy-start.21
  112.7 0.7 copy-start.34
  112.7 1.2 copy-start.30
  115.8 13.2 %copy-start.32 = (f32[256]{0:T(256)S(1)}, f32[256]{0:T(256)}, u32[]{:S(2)}) copy-start(f32[256]{0:T(256)} %param.20) | copy-start | bytes 3076
  129.0 47.7 %copy-start.26 = (bf16[2,2,13,128,1]{3,2,1,0,4:T(8,128)(2,1)S(1)}, bf16[2,2,13,128,1]{3,2,1,0,4:T(8,128)(2,1)}, u32[]{:S(2)}) copy-start(bf16[2,2,13,128,1]{3,2,1,0,4:T(8,128)(2,1)} %constant.67) | copy-start | bytes 39940
  135.1 42.1 %copy-start.22 = (f32[84,128]{1,0:T(8,128)S(1)}, f32[84,128]{1,0:T(8,128)}, u32[]{:S(2)}) copy-start(f32[84,128]{1,0:T(8,128)} %constant.64) | copy-start | bytes 129028
  177.4 1.3 copy-start.28
  179.8 2.4 %copy-start.11 = (f32[1,8,10752]{2,1,0:T(8,128)S(1)}, f32[1,8,10752]{2,1,0:T(8,128)}, u32[]{:S(2)}) copy-start(f32[1,8,10752]{2,1,0:T(8,128)} %get-tuple-element.44) | copy-start | bytes 1032196
  179.9 2.4 %copy-start.14 = (f32[1,8,10752]{2,1,0:T(8,128)S(1)}, f32[1,8,10752]{2,1,0:T(8,128)}, u32[]{:S(2)}) copy-start(f32[1,8,10752]{2,1,0:T(8,128)} %get-tuple-element.4) | copy-start | bytes 1032196
  180.7 6.2 %copy-start.6 = (f32[8,10752]{1,0:T(8,128)S(1)}, f32[8,10752]{1,0:T(8,128)}, u32[]{:S(2)}) copy-start(f32[8,10752]{1,0:T(8,128)} %param.17) | copy-start | bytes 1032196
  180.7 6.2 %copy-start.8 = (f32[8,10752]{1,0:T(8,128)S(1)}, f32[8,10752]{1,0:T(8,128)}, u32[]{:S(2)}) copy-start(f32[8,10752]{1,0:T(8,128)} %get-tuple-element.42) | copy-start | bytes 1032196
  180.7 6.2 %copy-start.10 = (f32[8,10752]{1,0:T(8,128)S(1)}, f32[8,10752]{1,0:T(8,128)}, u32[]{:S(2)}) copy-start(f32[8,10752]{1,0:T(8,128)} %get-tuple-element.43) | copy-start | bytes 1032196
  180.7 6.2 %copy-start.15 = (f32[8,10752]{1,0:T(8,128)S(1)}, f32[8,10752]{1,0:T(8,128)}, u32[]{:S(2)}) copy-start(f32[8,10752]{1,0:T(8,128)} %get-tuple-element.21) | copy-start | bytes 1032196
  180.7 6.2 %copy-start.16 = (f32[8,10752]{1,0:T(8,128)S(1)}, f32[8,10752]{1,0:T(8,128)}, u32[]{:S(2)}) copy-start(f32[8,10752]{1,0:T(8,128)} %get-tuple-element.40) | copy-start | bytes 1032196
  180.8 6.0 %collective-permute-start.4 = (bf16[1,10752]{1,0:T(2,128)(2,1)S(1)}, bf16[1,10752]{1,0:T(2,128)(2,1)S(1)}, u32[]{:S(2)}, u32[]{:S(2)}) collective-permute-start(bf16[1,10752]{1,0:T(2,128)(2,1)S(1)} %slice.436), channel_id=1, source_target_pairs={{4,0},{8,4},{12,8},{16,12},{20,16},{24,20},{28,24},{5,1},{9,5},{13... | collective-permute-start | bytes 64520 | tf_op jit(solution)/shard_map/ppermute | solution.py:16
  187.3 4.9 %collective-permute-start.5 = (bf16[1,10752]{1,0:T(2,128)(2,1)S(1)}, bf16[1,10752]{1,0:T(2,128)(2,1)S(1)}, u32[]{:S(2)}, u32[]{:S(2)}) collective-permute-start(bf16[1,10752]{1,0:T(2,128)(2,1)S(1)} %slice.435), channel_id=1, source_target_pairs={{0,4},{4,8},{8,12},{12,16},{16,20},{20,24},{24,28},{1,5},{5,9},{9,... | collective-permute-start | bytes 64520 | tf_op jit(solution)/shard_map/ppermute | solution.py:16
Sparse Core Ops, SparseCore 0:
  52.3 28.9 all-reduce.6
  135.2 27.9 all-reduce.8
where the time goes:
time: 201 us; the launch traced here: 200 us
  waiting for transfers between devices  79.5 us (40%)
  blocking collectives  35.2 us (18%)
  starting transfers between devices  20.9 us (10%)
  local copies, waits for them, and re-layouts  20.4 us (10%)
  between operations  15 us (7%)
  matrix products  14.8 us (7%)
  other arithmetic  14.2 us (7%)
    psum x2, waiting for transfers between devices, on_device(): total_sum = lax.psum(partial_value.astype(jnp.bfloat16), 'deg')  57.2 us
    all_to_all x2, blocking collectives, on_device(): lax.all_to_all(spectra, 'lat', split_axis=1, concat_axis=3, tiled=True)  23 us
    ppermute x6, waiting for transfers between devices, passed_along(): return lax.ppermute(value, axis, pairs)  15.4 us
    ppermute x6, starting transfers between devices, passed_along(): return lax.ppermute(value, axis, pairs)  15.3 us
    all_to_all x1, blocking collectives, on_device(): lax.all_to_all(total_sum, 'lat', split_axis=3, concat_axis=1, tiled=True)  12.2 us
    dot_general x2, matrix products, legendre(): jnp.einsum('cmfl,mil->cmfi', scaled, basis, preferred_element_type=jnp.fl...  12 us
    unnamed x74, local copies, waits for them, and re-layouts  8.38 us
    all_to_all x1, waiting for transfers between devices, on_device(): lax.all_to_all(total_sum, 'lat', split_axis=3, concat_axis=1, tiled=True)  6.85 us
  transfers between devices with their start and end apart: 9, of which 9 were waited for; matrix products, arithmetic and copies ran while one was open for 2% of the time, Pallas kernels for 0%

commit v1 on v0

--- a/solution.py
+++ b/solution.py
@@ -141,7 +141,11 @@
         owned_rows = lax.all_to_all(spectra, "lat", split_axis=1, concat_axis=3, tiled=True)
         partial_value = legendre(owned_rows, basis, love)
         total_sum = lax.psum(partial_value.astype(jnp.bfloat16), "deg")
-        banded = lax.all_to_all(total_sum, "lat", split_axis=3, concat_axis=1, tiled=True)
+        mixed_arr = lax.psum(1, "lat")
+        y = jnp.split(total_sum, mixed_arr, axis=3)
+        local_now = jnp.stack(y, axis=0)
+        o_now = lax.all_to_all(local_now, split_axis=0, concat_axis=0, axis_name="lat")
+        banded = jnp.concatenate(o_now, axis=1)
         loads = synthesise(banded, full_factor, tables, output_weight)
         last = step_index == STEPS - 1
         psi_now = state_eta - loads[0]

time: 201 us -> 212 us (1.055)
  local copies, waits for them, and re-layouts: 20.4 us -> 29 us
    another operation x0 -> x20, local copies, waits for them, and re-layouts: none -> 7.17 us  [on_device(): local_now = jnp.stack(y, axis=0)]
    unnamed x74 -> x88, local copies, waits for them, and re-layouts: 8.38 us -> 11.7 us
    psum x2 -> x0, local copies, waits for them, and re-layouts: 2.7 us -> none  [on_device(): total_sum = lax.psum(partial_value.astype(jnp.bfloat16), 'deg')]
where the time goes in v1:
time: 212 us; the launch traced here: 211 us
  waiting for transfers between devices  79.6 us (38%)
  blocking collectives  35.2 us (17%)
  local copies, waits for them, and re-layouts  29 us (14%)
  starting transfers between devices  20.9 us (10%)
  other arithmetic  16.1 us (8%)
  between operations  15 us (7%)
  matrix products  14.8 us (7%)
    psum x2, waiting for transfers between devices, on_device(): total_sum = lax.psum(partial_value.astype(jnp.bfloat16), 'deg')  57.3 us
    all_to_all x2, blocking collectives, on_device(): lax.all_to_all(spectra, 'lat', split_axis=1, concat_axis=3, tiled=True)  23 us
    ppermute x6, waiting for transfers between devices, passed_along(): return lax.ppermute(value, axis, pairs)  15.4 us
    ppermute x6, starting transfers between devices, passed_along(): return lax.ppermute(value, axis, pairs)  15.3 us
    all_to_all x1, blocking collectives, on_device(): lax.all_to_all(local_now, split_axis=0, concat_axis=0, axis_name='lat')  12.2 us
    dot_general x2, matrix products, legendre(): jnp.einsum('cmfl,mil->cmfi', scaled, basis, preferred_element_type=jnp.fl...  12 us
    unnamed x88, local copies, waits for them, and re-layouts  11.7 us
    another operation x20, local copies, waits for them, and re-layouts, on_device(): local_now = jnp.stack(y, axis=0)  7.17 us
  transfers between devices with their start and end apart: 9, of which 9 were waited for; matrix products, arithmetic and copies ran while one was open for 2% of the time, Pallas kernels for 0%

profile of v1, /device:TPU:0, one launch (start us, length us, event | category | flops | bytes accessed | tf_op | source)
XLA Modules:
  0.0 210.6 jit_solution(11826080757478202720)
XLA Ops:
  7.3 1.0 slice.442
  8.3 1.0 convert_element_type.99
  9.3 1.3 multiply_multiply_fusion.3
  10.8 1.3 collective-permute-start
  12.8 0.5 copy-done.4
  13.4 4.8 %collective-permute-done = bf16[3,10752]{1,0:T(4,128)(2,1)S(1)} collective-permute-done((bf16[3,10752]{1,0:T(4,128)(2,1)S(1)}, bf16[3,10752]{1,0:T(4,128)(2,1)S(1)}, u32[]{:S(2)}, u32[]{:S(2)}) %collective-permute-start) | collective-permute-done | bytes 64544 | tf_op jit(solution)/shard_map/ppermute | solution.py:16
  18.3 1.3 broadcast_multiply_fusion.3
  19.7 4.8 %collective-permute-start.1 = (bf16[1,10752]{1,0:T(2,128)(2,1)S(1)}, bf16[1,10752]{1,0:T(2,128)(2,1)S(1)}, u32[]{:S(2)}, u32[]{:S(2)}) collective-permute-start(bf16[1,10752]{1,0:T(2,128)(2,1)S(1)} %slice.440), channel_id=1, source_target_pairs={{0,4},{4,8},{8,12},{12,16},{16,20},{20,24},{24,28},{1,5},{5,9},{9,... | collective-permute-start | bytes 64520 | tf_op jit(solution)/shard_map/ppermute | solution.py:16
  24.6 1.6 collective-permute-done.1
  26.2 0.9 convert_bitcast_fusion.2
  27.4 0.3 convolution_bitcast_fusion.3
  28.2 0.5 copy-done.33
  28.7 0.4 convolution_bitcast_fusion.7
  29.3 0.7 copy.84
  30.0 1.1 reshape.120
  31.1 12.4 %all_to_all.46 = bf16[8,2,2048]{2,1,0:T(2,128)(2,1)S(1)} all-to-all(bf16[8,2,2048]{2,1,0:T(2,128)(2,1)S(1)} %reshape.120), channel_id=1, replica_groups=mesh['lat'=8,'deg'=4] {'lat'}, dimensions={0} | all-to-all | bytes 131072 | tf_op jit(solution)/shard_map/all_to_all | solution.py:141
  43.5 1.2 reshape.121
  44.7 1.3 copy.131
  46.2 6.0 %fusion.45 = bf16[2,128,2,64]{3,2,0,1:T(2,128)(2,1)} fusion(bf16[128,64,256]{2,1,0:T(8,128)(2,1)} %param.19, bf16[2,128,2,64]{3,2,0,1:T(2,128)(2,1)S(1)} %copy.87, f32[256]{0:T(256)S(1)} %copy-done.31), kind=kOutput, calls=%fused_computation.25 | convolution fusion | flops 33849344 | bytes 4326400 | tf_op jit(solution)/shard_map/cmfl,mil->cmfi/dot_general | solution.py:60
  52.2 29.1 %all-reduce.7.cloned.1.call-done = bf16[2,128,2,64]{3,2,0,1:T(2,128)(2,1)} async-done(((bf16[2,128,2,64]{3,2,0,1:T(2,128)(2,1)}), bf16[2,128,2,64]{3,2,0,1:T(2,128)(2,1)}) %all-reduce.7.cloned.1.call-update) | async-done | bytes 65552 | tf_op jit(solution)/shard_map/psum | solution.py:143
  81.3 2.6 %slice_bitcast_fusion.12 = (bf16[1,2,128,2,8]{4,3,1,2,0:T(2,128)(2,1)S(1)}, bf16[1,2,128,2,8]{4,3,1,2,0:T(2,128)(2,1)S(1)}, bf16[1,2,128,2,8]{4,3,1,2,0:T(2,128)...) fusion(bf16[2,128,2,64]{3,2,0,1:T(2,128)(2,1)} %all-reduce.7.cl, ...), kind=kLoop, calls=%fused_computation.148 | loop fusion | bytes 131072 | tf_op jit(solution)/shard_map/stack | solution.py:146
  84.6 0.6 constant_dynamic-update-slice_fusion.7
  85.2 0.6 constant_dynamic-update-slice_fusion.6
  85.8 0.6 constant_dynamic-update-slice_fusion.5
  86.4 0.6 constant_dynamic-update-slice_fusion.4
  87.0 0.6 constant_dynamic-update-slice_fusion.3
  87.6 0.6 constant_dynamic-update-slice_fusion.2
  88.2 0.6 constant_dynamic-update-slice_fusion.1
  88.8 0.6 constant_dynamic-update-slice_fusion
  89.4 5.5 %all-to-all-start.1 = ((bf16[8,2,128,2,8]{2,4,3,1,0:T(8,128)(2,1)}), bf16[8,2,128,2,8]{2,4,3,1,0:T(8,128)(2,1)S(1)}, u32[]{:S(2)}, u32[]{:S(2)}) async-start(bf16[8,2,128,2,8]{2,4,3,1,0:T(8,128)(2,1)} %constant_dynamic-update-slice_fusion), calls=%async_computation.1 | async-start | bytes 131072 | tf_op jit(solution)/shard_map/all_to_all | solution.py:147
  95.0 6.8 %all-to-all-done.1 = bf16[8,2,128,2,8]{2,4,3,1,0:T(8,128)(2,1)S(1)} async-done(((bf16[8,2,128,2,8]{2,4,3,1,0:T(8,128)(2,1)}), bf16[8,2,128,2,8]{2,4,3,1,0:T(8,128)(2,1)S(1)}, u32[]{:S(2)}, u32[]{:S(2)}) %all-to-all-start.1) | async-done | bytes 65568 | tf_op jit(solution)/shard_map/all_to_all | solution.py:147
  102.1 0.4 convolution_bitcast_fusion.2
  103.0 1.0 reshape.94
  104.0 1.3 broadcast_multiply_fusion.1
  105.6 0.7 copy-done.2
  106.4 1.3 collective-permute-start.2
  107.8 0.9 multiply_bitcast_fusion.1
  108.9 3.5 %collective-permute-done.2 = bf16[2,10752]{1,0:T(2,128)(2,1)S(1)} collective-permute-done((bf16[2,10752]{1,0:T(2,128)(2,1)S(1)}, bf16[2,10752]{1,0:T(2,128)(2,1)S(1)}, u32[]{:S(2)}, u32[]{:S(2)}) %collective-permute-start.2) | collective-permute-done | bytes 43040 | tf_op jit(solution)/shard_map/ppermute | solution.py:16
  112.4 1.3 fusion.128
  114.0 3.4 %collective-permute-start.3 = (bf16[2,10752]{1,0:T(2,128)(2,1)S(1)}, bf16[2,10752]{1,0:T(2,128)(2,1)S(1)}, u32[]{:S(2)}, u32[]{:S(2)}) collective-permute-start(bf16[2,10752]{1,0:T(2,128)(2,1)S(1)} %pad_maximum_fusion.6), channel_id=1, source_target_pairs={{0,4},{4,8},{8,12},{12,16},{16,20},{20,24},{24,28},{1,5},{5,9},{9,... | collective-permute-start | bytes 129032 | tf_op jit(solution)/shard_map/ppermute | solution.py:16
  117.5 1.3 collective-permute-done.3
  119.2 0.9 convert_bitcast_fusion
  121.1 0.5 copy-done.34
  121.6 0.4 convolution_bitcast_fusion.6
  122.2 0.7 copy.100
  123.0 1.1 reshape.122
  124.0 10.6 %all_to_all.47 = bf16[8,2,2048]{2,1,0:T(2,128)(2,1)S(1)} all-to-all(bf16[8,2,2048]{2,1,0:T(2,128)(2,1)S(1)} %reshape.122), channel_id=1, replica_groups=mesh['lat'=8,'deg'=4] {'lat'}, dimensions={0} | all-to-all | bytes 131072 | tf_op jit(solution)/shard_map/all_to_all | solution.py:141
  134.6 1.2 reshape.123
  135.8 1.3 copy.137
  137.3 6.0 %fusion.40 = bf16[2,128,2,64]{3,2,0,1:T(2,128)(2,1)} fusion(bf16[128,64,256]{2,1,0:T(8,128)(2,1)} %param.19, bf16[2,128,2,64]{3,2,0,1:T(2,128)(2,1)S(1)} %copy.103, f32[256]{0:T(256)S(1)} %copy-done.32), kind=kOutput, calls=%fused_computation.24 | convolution fusion | flops 33849344 | bytes 4326400 | tf_op jit(solution)/shard_map/cmfl,mil->cmfi/dot_general | solution.py:60
  143.3 28.2 %all-reduce.9.cloned.1.call-done = bf16[2,128,2,64]{3,2,0,1:T(2,128)(2,1)} async-done(((bf16[2,128,2,64]{3,2,0,1:T(2,128)(2,1)}), bf16[2,128,2,64]{3,2,0,1:T(2,128)(2,1)}) %all-reduce.9.cloned.1.call-update) | async-done | bytes 65552 | tf_op jit(solution)/shard_map/psum | solution.py:143
  171.5 2.6 %slice_bitcast_fusion.4 = (bf16[1,2,128,2,8]{4,3,1,2,0:T(2,128)(2,1)S(1)}, bf16[1,2,128,2,8]{4,3,1,2,0:T(2,128)(2,1)S(1)}, bf16[1,2,128,2,8]{4,3,1,2,0:T(2,128)(...) fusion(bf16[2,128,2,64]{3,2,0,1:T(2,128)(2,1)} %all-reduce.9.cl, ...), kind=kLoop, calls=%fused_computation.138 | loop fusion | bytes 131072 | tf_op jit(solution)/shard_map/stack | solution.py:146
  174.9 12.2 %all_to_all.48 = bf16[8,2,128,2,8]{2,4,3,1,0:T(8,128)(2,1)S(1)} all-to-all(bf16[8,2,128,2,8]{2,4,3,1,0:T(8,128)(2,1)S(1)} %constant_dynamic-update-slice_fusion.8), channel_id=1, replica_groups=mesh['lat'=8,'deg'=4] {'lat'}, dimensions={0} | all-to-all | bytes 131072 | tf_op jit(solution)/shard_map/all_to_all | solution.py:147
  187.3 0.4 convolution_bitcast_fusion
  188.3 1.0 reshape.99
  189.2 1.3 broadcast_multiply_fusion
  190.5 0.8 fusion.62
  191.4 1.4 collective-permute-start.4
  192.8 0.9 pad_maximum_fusion.1
  193.9 3.5 %collective-permute-done.4 = bf16[1,10752]{1,0:T(2,128)(2,1)S(1)} collective-permute-done((bf16[1,10752]{1,0:T(2,128)(2,1)S(1)}, bf16[1,10752]{1,0:T(2,128)(2,1)S(1)}, u32[]{:S(2)}, u32[]{:S(2)}) %collective-permute-start.4) | collective-permute-done | bytes 21536 | tf_op jit(solution)/shard_map/ppermute | solution.py:16
  197.9 3.2 %collective-permute-start.5 = (bf16[1,10752]{1,0:T(2,128)(2,1)S(1)}, bf16[1,10752]{1,0:T(2,128)(2,1)S(1)}, u32[]{:S(2)}, u32[]{:S(2)}) collective-permute-start(bf16[1,10752]{1,0:T(2,128)(2,1)S(1)} %slice.435), channel_id=1, source_target_pairs={{0,4},{4,8},{8,12},{12,16},{16,20},{20,24},{24,28},{1,5},{5,9},{9,... | collective-permute-start | bytes 64520 | tf_op jit(solution)/shard_map/ppermute | solution.py:16
  201.1 0.9 pad_maximum_fusion
  202.1 0.7 collective-permute-done.5
  202.8 0.9 fusion.101
  (167 shorter events, 8.7 us)
Async XLA Ops:
  7.2 74.1 %all-reduce.7.cloned.1.call-start = ((), (), s32[]{:S(2)}) async-start(), calls=%async_computation.4 | async-start | bytes 262144 | tf_op jit(solution)/shard_map/psum | solution.py:143
  9.3 3.1 %copy-start.1 = (f32[8,10752]{1,0:T(8,128)}, f32[8,10752]{1,0:T(8,128)S(1)}, u32[]{:S(2)}) copy-start(f32[8,10752]{1,0:T(8,128)S(1)} %convert_element_type.99) | copy-start | bytes 1032196
  9.3 3.0 %copy-start.3 = (f32[8,10752]{1,0:T(8,128)S(1)}, f32[8,10752]{1,0:T(8,128)}, u32[]{:S(2)}) copy-start(f32[8,10752]{1,0:T(8,128)} %param.16) | copy-start | bytes 1032196
  10.8 7.4 %collective-permute-start = (bf16[3,10752]{1,0:T(4,128)(2,1)S(1)}, bf16[3,10752]{1,0:T(4,128)(2,1)S(1)}, u32[]{:S(2)}, u32[]{:S(2)}) collective-permute-start(bf16[3,10752]{1,0:T(4,128)(2,1)S(1)} %pad_maximum_fusion.4), channel_id=1, source_target_pairs={{4,0},{8,4},{12,8},{16,12},{20,16},{24,20},{28,24},{5,1},{9,5},{13... | collective-permute-start | bytes 193544 | tf_op jit(solution)/shard_map/ppermute | solution.py:16
  12.4 1.0 copy-start.4
  12.5 5.8 %copy-start = (s32[8,10752]{1,0:T(8,128)S(1)}, s32[8,10752]{1,0:T(8,128)}, u32[]{:S(2)}) copy-start(s32[8,10752]{1,0:T(8,128)} %param.18) | copy-start | bytes 1032196
  12.5 5.8 %slice-start = ((f32[8,10752]{1,0:T(8,128)}), f32[8,1]{1,0:T(8,128)S(1)}, s32[]{:S(2)}) async-start(f32[8,10752]{1,0:T(8,128)} %copy-done.1), calls=%async_computation.6 | async-start | bytes 8192 | tf_op jit(solution)/shard_map/jit(_roll_static)/slice | solution.py:110
  12.5 5.8 %slice-start.1 = ((f32[8,10752]{1,0:T(8,128)}), f32[8,1]{1,0:T(8,128)S(1)}, s32[]{:S(2)}) async-start(f32[8,10752]{1,0:T(8,128)} %param.16), calls=%async_computation.7 | async-start | bytes 8192 | tf_op jit(solution)/shard_map/jit(_roll_static)/slice | solution.py:112
  12.6 5.8 %copy-start.23 = (f32[2,8,10752]{2,1,0:T(8,128)S(1)}, f32[2,8,10752]{2,1,0:T(8,128)}, u32[]{:S(2)}) copy-start(f32[2,8,10752]{2,1,0:T(8,128)} %param.15) | copy-start | bytes 2064388
  19.7 6.4 %collective-permute-start.1 = (bf16[1,10752]{1,0:T(2,128)(2,1)S(1)}, bf16[1,10752]{1,0:T(2,128)(2,1)S(1)}, u32[]{:S(2)}, u32[]{:S(2)}) collective-permute-start(bf16[1,10752]{1,0:T(2,128)(2,1)S(1)} %slice.440), channel_id=1, source_target_pairs={{0,4},{4,8},{8,12},{12,16},{16,20},{20,24},{24,28},{1,5},{5,9},{9,... | collective-permute-start | bytes 64520 | tf_op jit(solution)/shard_map/ppermute | solution.py:16
  24.5 4.7 %copy-start.29 = (f32[2,8]{1,0:T(2,128)}, f32[2,8]{1,0:T(2,128)S(1)}, u32[]{:S(2)}) copy-start(f32[2,8]{1,0:T(2,128)S(1)} %get-tuple-element.78) | copy-start | bytes 196
  24.5 79.5 %copy-start.27 = (f32[2,8]{1,0:T(2,128)}, f32[2,8]{1,0:T(2,128)S(1)}, u32[]{:S(2)}) copy-start(f32[2,8]{1,0:T(2,128)S(1)} %get-tuple-element.77) | copy-start | bytes 196
  26.2 1.2 copy-start.18
  27.1 0.8 copy-start.19
  27.1 0.8 copy-start.20
  28.0 0.7 copy-start.33
  31.1 15.1 %copy-start.31 = (f32[256]{0:T(256)S(1)}, f32[256]{0:T(256)}, u32[]{:S(2)}) copy-start(f32[256]{0:T(256)} %param.20) | copy-start | bytes 3076
  83.9 18.2 %copy-start.25 = (bf16[2,2,13,128,1]{3,2,1,0,4:T(8,128)(2,1)S(1)}, bf16[2,2,13,128,1]{3,2,1,0,4:T(8,128)(2,1)}, u32[]{:S(2)}) copy-start(bf16[2,2,13,128,1]{3,2,1,0,4:T(8,128)(2,1)} %constant.67) | copy-start | bytes 39940
  89.4 12.4 %all-to-all-start.1 = ((bf16[8,2,128,2,8]{2,4,3,1,0:T(8,128)(2,1)}), bf16[8,2,128,2,8]{2,4,3,1,0:T(8,128)(2,1)S(1)}, u32[]{:S(2)}, u32[]{:S(2)}) async-start(bf16[8,2,128,2,8]{2,4,3,1,0:T(8,128)(2,1)} %constant_dynamic-update-slice_fusion), calls=%async_computation.1 | async-start | bytes 131072 | tf_op jit(solution)/shard_map/all_to_all | solution.py:147
  94.9 76.5 %all-reduce.9.cloned.1.call-start = ((), (), s32[]{:S(2)}) async-start(), calls=%async_computation.5 | async-start | bytes 262144 | tf_op jit(solution)/shard_map/psum | solution.py:143
  103.9 1.3 copy-start.11
  104.0 1.3 copy-start.12
  105.3 1.0 copy-start.2
  105.3 2.5 %copy-start.5 = (f32[8,10752]{1,0:T(8,128)S(1)}, f32[8,10752]{1,0:T(8,128)}, u32[]{:S(2)}) copy-start(f32[8,10752]{1,0:T(8,128)} %param.17) | copy-start | bytes 1032196
  105.3 2.5 %copy-start.17 = (f32[8,10752]{1,0:T(8,128)S(1)}, f32[8,10752]{1,0:T(8,128)}, u32[]{:S(2)}) copy-start(f32[8,10752]{1,0:T(8,128)} %get-tuple-element.28) | copy-start | bytes 1032196
  106.4 5.9 %collective-permute-start.2 = (bf16[2,10752]{1,0:T(2,128)(2,1)S(1)}, bf16[2,10752]{1,0:T(2,128)(2,1)S(1)}, u32[]{:S(2)}, u32[]{:S(2)}) collective-permute-start(bf16[2,10752]{1,0:T(2,128)(2,1)S(1)} %pad_maximum_fusion.5), channel_id=1, source_target_pairs={{4,0},{8,4},{12,8},{16,12},{20,16},{24,20},{28,24},{5,1},{9,5},{13... | collective-permute-start | bytes 129032 | tf_op jit(solution)/shard_map/ppermute | solution.py:16
  108.6 3.8 %copy-start.6 = (f32[8,10752]{1,0:T(8,128)S(1)}, f32[8,10752]{1,0:T(8,128)}, u32[]{:S(2)}) copy-start(f32[8,10752]{1,0:T(8,128)} %get-tuple-element.42) | copy-start | bytes 1032196
  108.6 3.8 %copy-start.8 = (f32[8,10752]{1,0:T(8,128)S(1)}, f32[8,10752]{1,0:T(8,128)}, u32[]{:S(2)}) copy-start(f32[8,10752]{1,0:T(8,128)} %get-tuple-element.43) | copy-start | bytes 1032196
  108.6 3.8 %copy-start.24 = (f32[2,8,10752]{2,1,0:T(8,128)S(1)}, f32[2,8,10752]{2,1,0:T(8,128)}, u32[]{:S(2)}) copy-start(f32[2,8,10752]{2,1,0:T(8,128)} %param.13) | copy-start | bytes 2064388
  114.0 4.9 %collective-permute-start.3 = (bf16[2,10752]{1,0:T(2,128)(2,1)S(1)}, bf16[2,10752]{1,0:T(2,128)(2,1)S(1)}, u32[]{:S(2)}, u32[]{:S(2)}) collective-permute-start(bf16[2,10752]{1,0:T(2,128)(2,1)S(1)} %pad_maximum_fusion.6), channel_id=1, source_target_pairs={{0,4},{4,8},{8,12},{12,16},{16,20},{20,24},{24,28},{1,5},{5,9},{9,... | collective-permute-start | bytes 129032 | tf_op jit(solution)/shard_map/ppermute | solution.py:16
  120.1 0.8 copy-start.21
  120.9 0.7 copy-start.34
  120.9 1.2 copy-start.30
  124.0 13.2 %copy-start.32 = (f32[256]{0:T(256)S(1)}, f32[256]{0:T(256)}, u32[]{:S(2)}) copy-start(f32[256]{0:T(256)} %param.20) | copy-start | bytes 3076
  174.1 13.2 %copy-start.26 = (bf16[2,2,13,128,1]{3,2,1,0,4:T(8,128)(2,1)S(1)}, bf16[2,2,13,128,1]{3,2,1,0,4:T(8,128)(2,1)}, u32[]{:S(2)}) copy-start(bf16[2,2,13,128,1]{3,2,1,0,4:T(8,128)(2,1)} %constant.67) | copy-start | bytes 39940
  174.4 13.3 %copy-start.22 = (f32[84,128]{1,0:T(8,128)S(1)}, f32[84,128]{1,0:T(8,128)}, u32[]{:S(2)}) copy-start(f32[84,128]{1,0:T(8,128)} %constant.64) | copy-start | bytes 129028
  187.9 1.3 copy-start.28
  189.2 1.3 copy-start.13
  190.5 2.3 %copy-start.10 = (f32[1,8,10752]{2,1,0:T(8,128)S(1)}, f32[1,8,10752]{2,1,0:T(8,128)}, u32[]{:S(2)}) copy-start(f32[1,8,10752]{2,1,0:T(8,128)} %get-tuple-element.44) | copy-start | bytes 1032196
  190.5 2.3 %copy-start.14 = (f32[1,8,10752]{2,1,0:T(8,128)S(1)}, f32[1,8,10752]{2,1,0:T(8,128)}, u32[]{:S(2)}) copy-start(f32[1,8,10752]{2,1,0:T(8,128)} %get-tuple-element.4) | copy-start | bytes 1032196
  191.4 6.1 %copy-start.7 = (f32[8,10752]{1,0:T(8,128)S(1)}, f32[8,10752]{1,0:T(8,128)}, u32[]{:S(2)}) copy-start(f32[8,10752]{1,0:T(8,128)} %get-tuple-element.42) | copy-start | bytes 1032196
  191.4 6.1 %copy-start.9 = (f32[8,10752]{1,0:T(8,128)S(1)}, f32[8,10752]{1,0:T(8,128)}, u32[]{:S(2)}) copy-start(f32[8,10752]{1,0:T(8,128)} %get-tuple-element.43) | copy-start | bytes 1032196
  191.4 6.1 %copy-start.15 = (f32[8,10752]{1,0:T(8,128)S(1)}, f32[8,10752]{1,0:T(8,128)}, u32[]{:S(2)}) copy-start(f32[8,10752]{1,0:T(8,128)} %get-tuple-element.21) | copy-start | bytes 1032196
  191.4 6.1 %copy-start.16 = (f32[8,10752]{1,0:T(8,128)S(1)}, f32[8,10752]{1,0:T(8,128)}, u32[]{:S(2)}) copy-start(f32[8,10752]{1,0:T(8,128)} %get-tuple-element.40) | copy-start | bytes 1032196
  191.4 6.0 %collective-permute-start.4 = (bf16[1,10752]{1,0:T(2,128)(2,1)S(1)}, bf16[1,10752]{1,0:T(2,128)(2,1)S(1)}, u32[]{:S(2)}, u32[]{:S(2)}) collective-permute-start(bf16[1,10752]{1,0:T(2,128)(2,1)S(1)} %slice.436), channel_id=1, source_target_pairs={{4,0},{8,4},{12,8},{16,12},{20,16},{24,20},{28,24},{5,1},{9,5},{13... | collective-permute-start | bytes 64520 | tf_op jit(solution)/shard_map/ppermute | solution.py:16
  197.9 4.9 %collective-permute-start.5 = (bf16[1,10752]{1,0:T(2,128)(2,1)S(1)}, bf16[1,10752]{1,0:T(2,128)(2,1)S(1)}, u32[]{:S(2)}, u32[]{:S(2)}) collective-permute-start(bf16[1,10752]{1,0:T(2,128)(2,1)S(1)} %slice.435), channel_id=1, source_target_pairs={{0,4},{4,8},{8,12},{12,16},{16,20},{20,24},{24,28},{1,5},{5,9},{9,... | collective-permute-start | bytes 64520 | tf_op jit(solution)/shard_map/ppermute | solution.py:16
Sparse Core Ops, SparseCore 0:
  52.3 28.9 all-reduce.6
  143.4 27.9 all-reduce.8
